TPU v7x, 32 devices: a whole 2x2x4 slice. The times are simulated.
32 devices in a mesh: seq: 8 (over z, y), tr: 2 (over x), tc: 2 (over core).
Axes of the slice: x: 2, y: 2, z: 4, core: 2. Of those that a mesh axis runs over, the one named last changes fastest.
Arguments:
- activations: bfloat16 [8192, 1024], P('seq', ('tr', 'tc')), may hold values from -6 to 6
- seg_len: int32 [8], P('seq'), may hold values from 1 to 1024, as said below
- seg_start: int32 [8], P('seq'), may hold values from 0 to 1, as said below
- memory_rates: float32 [3, 8, 8], P(None, 'seq'), may hold values from 0 to 1, as said below
- w_qkv: bfloat16 [1024, 3, 1024], P(None, None, ('tr', 'tc')), may hold values from -0.1875 to 0.1875
- conv_w: float32 [4, 3, 1024], P(None, None, ('tr', 'tc')), may hold values from -3 to 3
- persistent: bfloat16 [2, 16, 1024], P(None, None, ('tr', 'tc')), may hold values from -6 to 6
- w_out: bfloat16 [1024, 1024], P(('tr', 'tc')), may hold values from -0.1875 to 0.1875
- w_gate: bfloat16 [1024, 2816], P(None, ('tr', 'tc')), may hold values from -0.1875 to 0.1875
- w_up: bfloat16 [1024, 2816], P(None, ('tr', 'tc')), may hold values from -0.1875 to 0.1875
- w_down: bfloat16 [2816, 1024], P(('tr', 'tc')), may hold values from -0.109375 to 0.109375
Outputs:
- layer_out: bfloat16 [8192, 1024], P('seq', ('tr', 'tc'))
Inputs may be any that keep to these rules, and one draw needn't show every extreme that they name: `seg_start`: 1 where a segment begins a prompt, 0 where it continues the prompt of the segment before; segment 0 begins a prompt; a prompt spans at most 4 segments, and in every draw one prompt spans exactly that many. `seg_len`: live tokens at the head of each segment; every segment of a prompt but its last is full. `memory_rates`: all three tables lie strictly between 0 and 1.
All inputs are finite; a program needn't handle non-finite values.
Results may differ from a plain program's by a relative error of at most 0.015.
Values may be sent and summed in bfloat16 or wider, within the bound.
A program may use at most 192 MiB of HBM per device.

v0:
```python
import jax
import jax.numpy as jnp
from jax import lax
from jax.sharding import PartitionSpec as P

HD = 128
SEG = 1024
CONV = 4


epsilon = 1e-06
score_scale = 8.0


def passed_along(block, axis, distance):
    devices = range(lax.axis_size(axis))
    route = [(i - distance, i) for i in devices if i - distance in devices]
    return lax.ppermute(block, axis, route)


def carried_in(array, axis, combine, identity):
    count, index = (lax.axis_size(axis), lax.axis_index(axis))
    everything = jax.tree.map(
        lambda part, kind: lax.all_gather(part.astype(kind), axis),
        array,
        (jnp.bfloat16, jnp.bfloat16),
    )
    start = jax.tree.map(
        lambda part, zero: jnp.broadcast_to(jnp.asarray(zero, part.dtype), part.shape),
        array,
        identity,
    )

    def step(k, before):
        reached = k < index
        new = combine(
            before, jax.tree.map(lambda part, own: part[k].astype(own.dtype), everything, array)
        )
        return jax.tree.map(lambda a, b: jnp.where(reached, a, b), new, before)

    return lax.fori_loop(0, count, step, start)


def unit_rows(values_in):
    return values_in * lax.rsqrt(jnp.sum(values_in * values_in, -1, keepdims=True) + epsilon)


def exact_product(left, right):
    return jnp.matmul(left, right, precision=lax.Precision.HIGHEST)


def combine(earlier, later):
    return (exact_product(later[0], earlier[0]), exact_product(later[0], earlier[1]) + later[1])


def body(
    activations,
    seg_len,
    seg_start,
    memory_rates,
    w_qkv,
    conv_w,
    persistent,
    w_out,
    w_gate,
    w_up,
    w_down,
):
    token_rows, local_feat = activations.shape
    seg_count = seg_len.shape[0]
    full_width = w_qkv.shape[0]
    head_width = w_qkv.shape[2]
    local_heads = head_width // HD
    group_index = lax.axis_index(("tr", "tc"))
    wide = w_qkv.reshape(full_width, 3 * head_width)
    row_ids = jnp.arange(token_rows, dtype=jnp.int32)
    position = row_ids % SEG
    segment_of = row_ids // SEG
    continuing = seg_start[segment_of] == 0
    piece = lax.all_gather(activations, ("tr", "tc"), axis=1, tiled=True)
    piece_f = piece.astype(jnp.float32)
    projected = jnp.dot(piece, wide, preferred_element_type=jnp.float32)
    squares = jnp.sum(piece_f * piece_f, -1)
    qkv = (projected * lax.rsqrt(squares / full_width + epsilon)[:, None]).astype(jnp.bfloat16)
    edge_rows = passed_along(qkv[token_rows - (CONV - 1) :], "seq", 1)
    extended = jnp.concatenate([edge_rows, qkv], 0)
    taps = conv_w.reshape(CONV, 3 * head_width)
    convolved = jnp.zeros((token_rows, 3 * head_width), jnp.float32)
    for offset in range(CONV):
        shifted = extended[CONV - 1 - offset : CONV - 1 - offset + token_rows].astype(jnp.float32)
        valid = (position >= offset) | continuing
        convolved = convolved + jnp.where(valid[:, None], taps[offset] * shifted, 0.0)
    parts = convolved.reshape(token_rows, 3, local_heads, HD)
    query_n = unit_rows(parts[:, 0]).astype(jnp.bfloat16)
    key_n = unit_rows(parts[:, 1]).astype(jnp.bfloat16)
    value_n = parts[:, 2].astype(jnp.bfloat16)
    pkeys = unit_rows(persistent[0].astype(jnp.float32).reshape(-1, local_heads, HD)).astype(
        jnp.bfloat16
    )
    pvalues = persistent[1].reshape(-1, local_heads, HD)
    persist_rows = pkeys.shape[0]
    live = position < seg_len[segment_of]
    keys_live = jnp.where(live[:, None, None], key_n, jnp.zeros((), jnp.bfloat16)).reshape(
        seg_count, SEG, local_heads, HD
    )
    value_segs = value_n.reshape(seg_count, SEG, local_heads, HD)
    a_mats = jnp.einsum("cthi,cthj->chij", keys_live, keys_live, preferred_element_type=jnp.float32)
    b_mats = jnp.einsum(
        "cthi,cthj->chij", keys_live, value_segs, preferred_element_type=jnp.float32
    )
    my_rates = lax.dynamic_slice_in_dim(memory_rates, group_index * local_heads, local_heads, 2)
    decay_factor = my_rates[0][:, :, None, None]
    eta = my_rates[1][:, :, None, None]
    theta = my_rates[2][:, :, None, None]
    keep = (1 - seg_start).astype(jnp.float32)[:, None, None, None]
    identity = jnp.eye(HD, dtype=jnp.float32)
    upper = jnp.concatenate([(1.0 - decay_factor) * identity - theta * a_mats, eta * identity], -1)
    lower = jnp.concatenate([-theta * a_mats, eta * identity], -1)
    seg_maps = jnp.concatenate([upper, lower], -2) * keep
    seg_shifts = jnp.concatenate([theta * b_mats, theta * b_mats], -2)
    dev_map = seg_maps[0]
    dev_shift = seg_shifts[0]
    neutral = (
        jnp.broadcast_to(jnp.eye(2 * HD, dtype=jnp.float32), dev_map.shape),
        jnp.zeros_like(dev_shift),
    )
    _, state = carried_in((dev_map, dev_shift), "seq", combine, neutral)
    seg_index = 0
    memory_in = state[:, :HD] * keep[seg_index]
    query_seg = query_n.astype(jnp.float32)
    retr_parts = jnp.einsum("thi,hij->thj", query_seg, memory_in, precision=lax.Precision.HIGHEST)
    mem = retr_parts * lax.rsqrt(jnp.mean(retr_parts * retr_parts, -1, keepdims=True) + epsilon)
    block_rows = min(512, SEG)
    attn_parts = []
    seg_index = 0
    first = seg_index * SEG
    keys_all = jnp.concatenate([pkeys, key_n], 0)
    values_all = jnp.concatenate([pvalues, value_n], 0)
    cols_k = jnp.arange(persist_rows + SEG, dtype=jnp.int32)[None, :] - persist_rows
    for block_start in range(0, SEG, block_rows):
        query_blk = query_n[first + block_start : first + block_start + block_rows]
        scores = score_scale * jnp.einsum(
            "qhd,khd->hqk", query_blk, keys_all, preferred_element_type=jnp.float32
        )
        rows_q = block_start + jnp.arange(block_rows, dtype=jnp.int32)[:, None]
        allow = (cols_k < 0) | (cols_k <= rows_q) & (cols_k < seg_len[seg_index])
        weights = jnp.where(allow[None], jnp.exp(scores), 0.0)
        probs = (weights / jnp.sum(weights, -1, keepdims=True)).astype(jnp.bfloat16)
        attn_parts.append(
            jnp.einsum("hqk,khd->qhd", probs, values_all, preferred_element_type=jnp.float32)
        )
    attn = jnp.concatenate(attn_parts, 0)
    heads_out = (attn + mem).astype(jnp.bfloat16).reshape(token_rows, head_width)
    partial_value = jnp.dot(heads_out, w_out, preferred_element_type=jnp.float32)
    share = lax.psum_scatter(
        partial_value.astype(jnp.bfloat16), ("tr", "tc"), scatter_dimension=1, tiled=True
    ).astype(jnp.float32)
    resid = (activations.astype(jnp.float32) + share).astype(jnp.bfloat16)
    piece = lax.all_gather(resid, ("tr", "tc"), axis=1, tiled=True)
    piece_f = piece.astype(jnp.float32)
    gate = jnp.dot(piece, w_gate, preferred_element_type=jnp.float32)
    up_proj = jnp.dot(piece, w_up, preferred_element_type=jnp.float32)
    squares2 = jnp.sum(piece_f * piece_f, -1)
    inv_rms2 = lax.rsqrt(squares2 / full_width + epsilon)[:, None]
    hidden = (jax.nn.silu(gate * inv_rms2) * (up_proj * inv_rms2)).astype(jnp.bfloat16)
    down = jnp.dot(hidden, w_down, preferred_element_type=jnp.float32)
    ffn_share = lax.psum_scatter(
        down.astype(jnp.bfloat16), ("tr", "tc"), scatter_dimension=1, tiled=True
    ).astype(jnp.float32)
    return (resid.astype(jnp.float32) + ffn_share).astype(jnp.bfloat16)


def solution(mesh):
    return jax.shard_map(
        body,
        mesh=mesh,
        in_specs=(
            P("seq", ("tr", "tc")),
            P("seq"),
            P("seq"),
            P(None, "seq", None),
            P(None, None, ("tr", "tc")),
            P(None, None, ("tr", "tc")),
            P(None, None, ("tr", "tc")),
            P(("tr", "tc"), None),
            P(None, ("tr", "tc")),
            P(None, ("tr", "tc")),
            P(("tr", "tc"), None),
        ),
        out_specs=P("seq", ("tr", "tc")),
        check_vma=False,
    )
```

profile of v0, /device:TPU:0, one launch (start us, length us, event | category | flops | bytes accessed | tf_op | source)
XLA Modules:
  0.0 278.3 jit_solution(17174360944193848645)
XLA Ops:
  6.5 0.7 all-gather.5.cloned.1.call-update
  7.3 0.0 all-gather.9.cloned.1.call-start
  8.6 2.6 copy.46
  11.3 23.2 %all-gather.5.cloned.1.call-done = bf16[1024,1024]{1,0:T(8,128)(2,1)} async-done(((bf16[1024,256]{1,0:T(8,128)(2,1)}), bf16[1024,1024]{1,0:T(8,128)(2,1)}) %all-gather.5.cloned.1.call-update) | async-done | bytes 2097168 | tf_op jit(solution)/shard_map/all_gather | solution.py:80
  34.5 2.1 multiply_reduce_fusion.1
  36.6 3.9 %multiply_convert_fusion = bf16[1024,768]{1,0:T(8,128)(2,1)S(1)} fusion(bf16[1024,1024]{1,0:T(8,128)(2,1)} %all-gather.5.cloned.1.call-done, bf16[1024,768]{0,1:T(8,128)(2,1)} %bitcast.65, f32[1024]{0:T(1024)S(1)} %add_rsqrt_fusion.4), kind=kOutput, calls=%fused_computation.20 | convolution fusion | flops 1612185600 | bytes 5246976 | tf_op jit(solution)/shard_map/dot_general | solution.py:82
  40.5 3.4 %collective-permute-start = (bf16[3,768]{1,0:T(4,128)(2,1)S(1)}, bf16[3,768]{1,0:T(4,128)(2,1)S(1)}, u32[]{:S(2)}, u32[]{:S(2)}) collective-permute-start(bf16[3,768]{1,0:T(4,128)(2,1)S(1)} %slice.81), channel_id=1, source_target_pairs={{0,4},{4,8},{8,12},{12,16},{16,20},{20,24},{24,28},{1,5},{5,9},{9,... | collective-permute-start | bytes 13832 | tf_op jit(solution)/shard_map/ppermute | solution.py:18
  43.9 0.1 fusion.60
  44.0 1.2 collective-permute-done
  45.2 3.8 %select_add_fusion = f32[1024,768]{1,0:T(8,128)} fusion(bf16[1024,768]{1,0:T(8,128)(2,1)S(1)} %multiply_convert_fusion, bf16[3,768]{1,0:T(4,128)(2,1)S(1)} %collective-permute-done, f32[768]{0:T(1024)S(1)} %mul.256, f32[768]{0:T(1024)S(1)} %mul.253, f32[768]{0:T(1024)S(1)} %mul.250, f32[768]{0:T(1024)S(1)} %mul.244, ...), kind=kLoop, calls=%fused_computation.19 | loop fusion | flops 18874368 | bytes 4739584 | tf_op jit(solution)/shard_map/add | solution.py:92
  49.0 5.2 %reshape.355 = f32[1024,3,2,128]{3,2,1,0:T(2,128)} reshape(f32[1024,768]{1,0:T(8,128)} %select_add_fusion) | data formatting | bytes 6291456 | tf_op jit(solution)/shard_map/reshape | solution.py:93
  54.2 1.6 slice.86
  55.8 1.7 fusion.62
  57.5 0.1 copy.81
  57.6 0.4 multiply_reduce_fusion.3
  57.9 0.3 multiply_convert_fusion.2
  58.3 0.1 copy-done.7
  58.4 0.5 fusion.23
  58.9 0.8 copy.57
  59.7 0.0 all-gather.9.cloned.1.call-update
  59.7 0.0 all-gather.7.cloned.1.call-start
  59.7 0.1 fusion.49
  59.8 0.1 broadcast_multiply_fusion
  59.9 0.6 subtract_bitcast_fusion
  60.6 0.9 copy.54
  61.5 0.0 all-gather.7.cloned.1.call-update
  61.5 0.2 reduce-scatter.3.cloned.1.call-start
  61.8 0.1 multiply_reduce_fusion.5
  61.9 0.1 copy.50
  62.0 0.1 fusion.32
  62.1 2.1 fusion.15
  64.2 0.4 multiply_reduce_fusion.4
  64.6 0.3 multiply_convert_fusion.3
  65.0 2.9 %fusion.11 = f32[2,512,1040]{1,2,0:T(8,128)} fusion(pred[512,1040]{0,1:T(8,128)(4,1)S(1)} %get-tuple-element.151, bf16[1024,2,128]{2,0,1:T(8,128)(2,1)S(1)} %copy-done.5, bf16[16,2,128]{2,0,1:T(8,128)(2,1)S(1)} %fusion.32, bf16[1024,2,128]{2,0,1:T(8,128)(2,1)S(1)} %multiply_convert_fusion.3), kind=kOutput, calls=%fused_computation.14 | convolution fusion | flops 275824640 | bytes 5586944 | tf_op jit(solution)/shard_map/qhd,khd->hqk/dot_general | solution.py:142
  67.9 5.5 %fusion.20 = f32[512,2,128]{0,2,1:T(8,128)} fusion(f32[2,512,1040]{1,2,0:T(8,128)} %fusion.11, bf16[1024,2,128]{2,0,1:T(8,128)(2,1)} %bitcast.67, bf16[16,2,128]{2,0,1:T(8,128)(2,1)S(1)} %copy.48), kind=kOutput, calls=%fused_computation.38 | convolution fusion | flops 275826688 | bytes 5316608 | tf_op jit(solution)/shard_map/hqk,khd->qhd/dot_general | solution.py:150
  73.4 4.0 %fusion.9 = f32[2,512,1040]{1,2,0:T(8,128)} fusion(pred[512,1040]{0,1:T(8,128)(4,1)S(1)} %copy-done.3, bf16[1024,2,128]{2,0,1:T(8,128)(2,1)} %copy-done.4, bf16[16,2,128]{2,0,1:T(8,128)(2,1)S(1)} %fusion.32, bf16[1024,2,128]{2,0,1:T(8,128)(2,1)S(1)} %multiply_convert_fusion.3), kind=kOutput, calls=%fused_computation.12 | convolution fusion | flops 275824640 | bytes 5586944 | tf_op jit(solution)/shard_map/qhd,khd->hqk/dot_general | solution.py:142
  77.3 5.3 %fusion.21 = f32[512,2,128]{0,2,1:T(8,128)} fusion(f32[2,512,1040]{1,2,0:T(8,128)} %fusion.9, bf16[1024,2,128]{2,0,1:T(8,128)(2,1)} %bitcast.68, bf16[16,2,128]{2,0,1:T(8,128)(2,1)S(1)} %copy.48), kind=kOutput, calls=%fused_computation.39 | convolution fusion | flops 275826688 | bytes 5316608 | tf_op jit(solution)/shard_map/hqk,khd->qhd/dot_general | solution.py:150
  82.7 18.2 %all-gather.9.cloned.1.call-done = bf16[8,2,256,128]{3,2,1,0:T(8,128)(2,1)} async-done(((bf16[1,2,256,128]{3,2,1,0:T(8,128)(2,1)}), bf16[8,2,256,128]{3,2,1,0:T(8,128)(2,1)}) %all-gather.9.cloned.1.call-update) | async-done | bytes 1048592 | tf_op jit(solution)/shard_map/all_gather | solution.py:24
  100.9 50.2 %all-gather.7.cloned.1.call-done = bf16[8,2,256,256]{3,2,1,0:T(8,128)(2,1)} async-done(((bf16[1,2,256,256]{3,2,1,0:T(8,128)(2,1)}), bf16[8,2,256,256]{3,2,1,0:T(8,128)(2,1)}) %all-gather.7.cloned.1.call-update) | async-done | bytes 2097168 | tf_op jit(solution)/shard_map/all_gather | solution.py:24
  151.1 11.7 %while.14 = (s32[]{:T(128)}, f32[2,256,128]{2,1,0:T(8,128)S(1)}, s32[]{:T(128)}, bf16[8,2,256,256]{3,2,1,0:T(8,128)(2,1)}, bf16[8,2,256,128]{3,2,1,0:T(8,128)(2,1)}, /*index=5*/s32[]{:T(128)}, s32[]{:T(128)}) while((s32[]{:T(128)}, f32[2,256,128]{2,1,0:T(8,128)S(1)}, s32[]{:T(128)}, bf16[8,2,256,256]{3,2,1,0:T(8,128)(2,1)}, ...), condition=%wide.region_7.8_spmd.clone, body=%wide.region_6.7_spmd.clone.sunk | while | flops 201654272 | bytes 1706599 | solution.py:41
  151.1 1.5 fusion.83
  152.6 1.4 fusion.83
  154.1 1.4 fusion.83
  155.5 1.4 fusion.83
  157.0 1.4 fusion.83
  158.4 1.4 fusion.83
  159.9 1.4 fusion.83
  161.3 1.4 fusion.83
  162.8 0.1 copy.58
  162.9 0.6 multiply_reduce_fusion.2
  163.6 1.3 fusion.24
  164.8 3.2 %convolution_convert_fusion = bf16[1024,1024]{1,0:T(8,128)(2,1)} fusion(bf16[1024,256]{0,1:T(8,128)(2,1)S(1)} %bitcast.64, bf16[256,1024]{1,0:T(8,128)(2,1)} %param.20), kind=kOutput, calls=%fused_computation.30 | convolution fusion | flops 537919488 | bytes 3145728 | tf_op jit(solution)/shard_map/dot_general | solution.py:154
  168.0 0.0 reduce-scatter.3.cloned.1.call-update
  168.1 0.0 all-gather.11.cloned.1.call-start
  168.1 30.0 %reduce-scatter.3.cloned.1.call-done = bf16[1024,256]{1,0:T(8,128)(2,1)} async-done(((bf16[1024,1024]{1,0:T(8,128)(2,1)}), bf16[1024,256]{1,0:T(8,128)(2,1)}) %reduce-scatter.3.cloned.1.call-update) | async-done | bytes 524304 | tf_op jit(solution)/shard_map/reduce_scatter | solution.py:155
  198.1 2.0 add_convert_fusion.1
  200.1 0.0 all-gather.11.cloned.1.call-update
  200.1 0.3 reduce-scatter.5.cloned.1.call-start
  200.4 22.7 %all-gather.11.cloned.1.call-done = bf16[1024,1024]{1,0:T(8,128)(2,1)} async-done(((bf16[1024,256]{1,0:T(8,128)(2,1)}), bf16[1024,1024]{1,0:T(8,128)(2,1)}) %all-gather.11.cloned.1.call-update) | async-done | bytes 2097168 | tf_op jit(solution)/shard_map/all_gather | solution.py:159
  223.1 2.1 multiply_reduce_fusion
  225.2 4.9 %fusion.64 = f32[1024,704]{0,1:T(8,128)} fusion(bf16[1024,1024]{1,0:T(8,128)(2,1)} %all-gather.11.cloned.1.call-done, bf16[1024,704]{0,1:T(8,128)(2,1)S(1)} %copy-done.11), kind=kOutput, calls=%fused_computation.123 | convolution fusion | flops 1476395008 | bytes 6422528 | tf_op jit(solution)/shard_map/dot_general | solution.py:161
  230.1 7.8 %convolution_convert_fusion.1 = bf16[1024,1024]{1,0:T(8,128)(2,1)} fusion(bf16[704,1024]{1,0:T(8,128)(2,1)S(1)} %copy-done, f32[1024,704]{0,1:T(8,128)} %fusion.64, bf16[1024,1024]{1,0:T(8,128)(2,1)} %all-gather.11.cloned.1.call-done, bf16[1024,704]{0,1:T(8,128)(2,1)} %param.22, f32[1024]{0:T(1024)S(1)} %add_rsqrt_fusion.3), kind=kOutput, calls=%fused_computation.31 | convolution fusion | flops 2959605760 | bytes 9965568 | tf_op jit(solution)/shard_map/dot_general | solution.py:166
  237.9 31.6 %reduce-scatter.5.cloned.1.call-done = bf16[1024,256]{1,0:T(8,128)(2,1)} async-done(((bf16[1024,1024]{1,0:T(8,128)(2,1)}), bf16[1024,256]{1,0:T(8,128)(2,1)}) %reduce-scatter.5.cloned.1.call-update) | async-done | bytes 524304 | tf_op jit(solution)/shard_map/reduce_scatter | solution.py:167
  269.5 2.0 add_convert_fusion
  (59 shorter events, 0.5 us)
Async XLA Ops:
  6.5 223.6 %copy-start = (bf16[704,1024]{1,0:T(8,128)(2,1)S(1)}, bf16[704,1024]{1,0:T(8,128)(2,1)}, u32[]{:S(2)}) copy-start(bf16[704,1024]{1,0:T(8,128)(2,1)} %param.23) | copy-start | bytes 4325380
  6.5 4.7 %copy-start.9 = (f32[4,3,256]{2,0,1:T(4,128)S(1)}, f32[4,3,256]{2,0,1:T(4,128)}, u32[]{:S(2)}) copy-start(f32[4,3,256]{2,0,1:T(4,128)} %param.18) | copy-start | bytes 36868
  6.5 27.9 %all-gather.5.cloned.1.call-start = ((), (), s32[]{:S(2)}) async-start(), calls=%async_computation.2 | async-start | bytes 2621440 | tf_op jit(solution)/shard_map/all_gather | solution.py:80
  7.3 93.6 %all-gather.9.cloned.1.call-start = ((), (), s32[]{:S(2)}) async-start(), calls=%async_computation.4 | async-start | bytes 1179648 | tf_op jit(solution)/shard_map/all_gather | solution.py:24
  36.6 7.3 %copy-start.10 = (f32[3,1,8]{2,1,0:T(1,128)S(1)}, f32[3,1,8]{2,1,0:T(1,128)}, u32[]{:S(2)}) copy-start(f32[3,1,8]{2,1,0:T(1,128)} %param.16) | copy-start | bytes 292
  40.5 4.7 %collective-permute-start = (bf16[3,768]{1,0:T(4,128)(2,1)S(1)}, bf16[3,768]{1,0:T(4,128)(2,1)S(1)}, u32[]{:S(2)}, u32[]{:S(2)}) collective-permute-start(bf16[3,768]{1,0:T(4,128)(2,1)S(1)} %slice.81), channel_id=1, source_target_pairs={{0,4},{4,8},{8,12},{12,16},{16,20},{20,24},{24,28},{1,5},{5,9},{9,... | collective-permute-start | bytes 13832 | tf_op jit(solution)/shard_map/ppermute | solution.py:18
  57.5 0.8 copy-start.7
  58.3 2.3 copy-start.4
  58.3 3.5 %copy-start.8 = (bf16[2,16,256]{2,1,0:T(8,128)(2,1)S(1)}, bf16[2,16,256]{2,1,0:T(8,128)(2,1)}, u32[]{:S(2)}) copy-start(bf16[2,16,256]{2,1,0:T(8,128)(2,1)} %param.19) | copy-start | bytes 49156
  59.7 91.4 %all-gather.7.cloned.1.call-start = ((), (), s32[]{:S(2)}) async-start(), calls=%async_computation.3 | async-start | bytes 2359296 | tf_op jit(solution)/shard_map/all_gather | solution.py:24
  61.5 136.6 %reduce-scatter.3.cloned.1.call-start = ((), (), s32[]{:S(2)}) async-start(), calls=%async_computation.5 | async-start | bytes 2621440 | tf_op jit(solution)/shard_map/reduce_scatter | solution.py:155
  62.0 3.0 %copy-start.5 = (bf16[1024,2,128]{2,0,1:T(8,128)(2,1)S(1)}, bf16[1024,2,128]{2,0,1:T(8,128)(2,1)}, u32[]{:S(2)}) copy-start(bf16[1024,2,128]{2,0,1:T(8,128)(2,1)} %copy-done.4) | copy-start | bytes 1572868
  67.9 5.5 %copy-start.3 = (pred[512,1040]{0,1:T(8,128)(4,1)S(1)}, pred[512,1040]{0,1:T(8,128)(4,1)}, u32[]{:S(2)}) copy-start(pred[512,1040]{0,1:T(8,128)(4,1)} %get-tuple-element.150) | copy-start | bytes 1597444
  151.1 12.5 %copy-start.6 = (f32[512,2,128]{0,2,1:T(8,128)S(1)}, f32[512,2,128]{0,2,1:T(8,128)}, u32[]{:S(2)}) copy-start(f32[512,2,128]{0,2,1:T(8,128)} %fusion.20) | copy-start | bytes 1572868
  164.8 33.3 %copy-start.2 = (bf16[1024,256]{1,0:T(8,128)(2,1)S(1)}, bf16[1024,256]{1,0:T(8,128)(2,1)}, u32[]{:S(2)}) copy-start(bf16[1024,256]{1,0:T(8,128)(2,1)} %param.13) | copy-start | bytes 1572868
  168.0 57.1 %copy-start.11 = (bf16[1024,704]{0,1:T(8,128)(2,1)S(1)}, bf16[1024,704]{0,1:T(8,128)(2,1)}, u32[]{:S(2)}) copy-start(bf16[1024,704]{0,1:T(8,128)(2,1)} %param.21) | copy-start | bytes 4325380
  168.1 55.0 %all-gather.11.cloned.1.call-start = ((), (), s32[]{:S(2)}) async-start(), calls=%async_computation.6 | async-start | bytes 2621440 | tf_op jit(solution)/shard_map/all_gather | solution.py:159
  200.1 69.4 %reduce-scatter.5.cloned.1.call-start = ((), (), s32[]{:S(2)}) async-start(), calls=%async_computation.7 | async-start | bytes 2621440 | tf_op jit(solution)/shard_map/reduce_scatter | solution.py:167
  230.1 39.4 %copy-start.1 = (bf16[1024,256]{1,0:T(8,128)(2,1)S(1)}, bf16[1024,256]{1,0:T(8,128)(2,1)}, u32[]{:S(2)}) copy-start(bf16[1024,256]{1,0:T(8,128)(2,1)} %add_convert_fusion.1) | copy-start | bytes 1572868
Sparse Core Ops, SparseCore 0:
  8.9 25.5 all-gather.4
  59.8 41.0 all-gather.8
  103.0 48.0 all-gather.6
  168.2 29.8 reduce-scatter.2
  200.2 22.8 all-gather.10
  238.0 31.4 reduce-scatter.4
where the time goes:
time: 279 us; the launch traced here: 278 us
  waiting for transfers between devices  178 us (64%)
  matrix products  50.4 us (18%)
  other arithmetic  17.2 us (6%)
  between operations  15.1 us (5%)
  local copies, waits for them, and re-layouts  13.4 us (5%)
  starting transfers between devices  3.99 us (1%)
    all_gather x2, waiting for transfers between devices, carried_in(): lax.all_gather(part.astype(kind), axis)  68.4 us
    reduce_scatter x1, waiting for transfers between devices, body(): lax.psum_scatter(down.astype(jnp.bfloat16), ('tr', 'tc'), scatter_dimensi...  31.6 us
    reduce_scatter x1, waiting for transfers between devices, body(): lax.psum_scatter(partial_value.astype(jnp.bfloat16), ('tr', 'tc'), scatte...  30 us
    all_gather x1, waiting for transfers between devices, body(): piece = lax.all_gather(activations, ('tr', 'tc'), axis=1, tiled=True)  23.2 us
    all_gather x1, waiting for transfers between devices, body(): piece = lax.all_gather(resid, ('tr', 'tc'), axis=1, tiled=True)  22.7 us
    dot_general x8, matrix products, exact_product(): return jnp.matmul(left, right, precision=lax.Precision.HIGHEST)  11.2 us
    dot_general x2, matrix products, body(): jnp.einsum('hqk,khd->qhd', probs, values_all, preferred_element_type=jnp....  10.8 us
    dot_general x1, matrix products, body(): down = jnp.dot(hidden, w_down, preferred_element_type=jnp.float32)  7.79 us
  transfers between devices with their start and end apart: 7, of which 7 were waited for; matrix products, arithmetic and copies ran while one was open for 9% of the time, Pallas kernels for 0%

commit v1 on v0

v1 whole, which is shorter than its diff:
```python
import functools

import jax
import jax.numpy as jnp
from jax import lax
from jax.experimental import pallas as pl
from jax.experimental.pallas import tpu as pltpu
from jax.sharding import PartitionSpec as P

HD = 128
SEG = 1024
CONV = 4
NC = 4
CR = SEG // NC
EPS = 1e-06
MESH = pl.DeviceIdType.MESH
F32 = jnp.float32
BF16 = jnp.bfloat16


def mm(a, b):
    return jnp.dot(a, b, preferred_element_type=F32)


def mm_t(a, b):
    return lax.dot_general(a, b, (((1,), (1,)), ((), ())), preferred_element_type=F32)


def unit_rows(v):
    return v * lax.rsqrt(jnp.sum(v * v, -1, keepdims=True) + EPS)


def split2(v):
    hi = v.astype(BF16)
    return hi, (v - hi.astype(F32)).astype(BF16)


def kernel(
    n_seq,
    span,
    len_ref,
    start_ref,
    rates_ref,
    x_ref,
    wqkv_ref,
    conv_ref,
    pers_ref,
    wout_ref,
    wgate_ref,
    wup_ref,
    wdown_ref,
    out_ref,
    xg,
    ext,
    edge_out,
    edge_in,
    qb,
    kb,
    va,
    pkb,
    pva,
    attn,
    packet,
    states,
    wog,
    hog,
    resid0,
    part0,
    part2,
    rs1_out,
    rs1_in,
    rs2_out,
    rs2_in,
    xs_s, xs_r, xx_s, xx_r, xf_s, xf_r,
    ws_s, ws_r,
    hs_s, hs_r, hx_s, hx_r, hf_s, hf_r,
    ed_s, ed_r,
    st_s, st_r,
    r1_s, r1_r, r2_s, r2_r,
):
    seq, tr, tc = lax.axis_index("seq"), lax.axis_index("tr"), lax.axis_index("tc")
    sib = (seq, tr, 1 - tc)
    xnb = (seq, 1 - tr, tc)
    d_model = 4 * 256
    group = (tr * 2 + tc, tr * 2 + 1 - tc, (1 - tr) * 2 + tc, (1 - tr) * 2 + 1 - tc)
    cols = [pl.ds(pl.multiple_of(g * 256, 256), 256) for g in group]

    def ahead(d):
        return (lax.rem(seq + d, n_seq), tr, tc)

    def send(src, dst, ssem, rsem, dev):
        return pltpu.make_async_remote_copy(
            src_ref=src, dst_ref=dst, send_sem=ssem, recv_sem=rsem, device_id=dev, device_id_type=MESH
        )

    barrier = pltpu.get_barrier_semaphore()
    peers = [sib, xnb] + [ahead(d) for d in range(1, span)] + [ahead(n_seq - d) for d in range(1, span)]
    for peer in peers:
        pl.semaphore_signal(barrier, inc=1, device_id=peer, device_id_type=MESH)
    pl.semaphore_wait(barrier, len(peers))

    def x_sib(c):
        return send(x_ref.at[c], xg.at[0, c], xs_s.at[c], xs_r.at[c], sib)

    def x_xnb(c):
        return send(x_ref.at[c], xg.at[1, c], xx_s.at[c], xx_r.at[c], xnb)

    def x_fwd(c):
        return send(xg.at[1, c], xg.at[2, c], xf_s.at[c], xf_r.at[c], sib)

    def h_sib(c):
        return send(hog.at[0, c], hog.at[1, c], hs_s.at[c], hs_r.at[c], sib)

    def h_xnb(c):
        return send(hog.at[0, c], hog.at[2, c], hx_s.at[c], hx_r.at[c], xnb)

    def h_fwd(c):
        return send(hog.at[2, c], hog.at[3, c], hf_s.at[c], hf_r.at[c], sib)

    def rs1(c):
        return send(rs1_out.at[c], rs1_in.at[c], r1_s.at[c], r1_r.at[c], sib)

    def rs2(c):
        return send(rs2_out.at[c], rs2_in.at[c], r2_s.at[c], r2_r.at[c], xnb)

    w_sib = send(wout_ref, wog.at[0], ws_s.at[0], ws_r.at[0], sib)
    w_xnb = send(wout_ref, wog.at[1], ws_s.at[1], ws_r.at[1], xnb)
    w_fwd = send(wog.at[1], wog.at[2], ws_s.at[2], ws_r.at[2], sib)
    edge = send(edge_out, edge_in, ed_s, ed_r, ahead(1))

    def state(d):
        return send(packet, states.at[d - 1], st_s.at[d - 1], st_r.at[d - 1], ahead(d))

    order = (NC - 1,) + tuple(range(NC - 1))
    for c in order:
        x_xnb(c).start()
        x_sib(c).start()

    length = len_ref[0]
    continuing = start_ref[0] == 0
    keep = jnp.where(continuing, 1.0, 0.0).astype(F32)

    pkb[...] = jnp.zeros_like(pkb)
    pva[...] = jnp.zeros_like(pva)
    for h in range(2):
        lanes = slice(h * HD, (h + 1) * HD)
        pkb[h, 0:16, :] = unit_rows(pers_ref[0, :, lanes].astype(F32)).astype(BF16)
        pva[h, 0:16, 0:HD] = pers_ref[1, :, lanes]
        pva[h, 0:16, HD:] = jnp.ones((16, HD), BF16)

    def wq(t):
        return wqkv_ref[pl.ds(pl.multiple_of(group[t] * 256, 256), 256), :]

    def rows8(c):
        return pl.ds(pl.multiple_of(8 + c * CR, 8), CR)

    def first_half(i, _):
        c = lax.rem(i + NC - 1, NC)
        x_sib(c).wait_recv()
        ext[rows8(c), :] = mm(x_ref[c], wq(0)) + mm(xg[0, c], wq(1))
        return 0

    lax.fori_loop(0, NC, first_half, 0)

    def sumsq(v):
        v = v.astype(F32)
        return jnp.sum(v * v, -1, keepdims=True)

    def second_half(i, _):
        c = lax.rem(i + NC - 1, NC)
        x_xnb(c).wait_recv()
        x_fwd(c).start()
        acc = ext[rows8(c), :] + mm(xg[1, c], wq(2))
        sq = sumsq(x_ref[c]) + sumsq(xg[0, c]) + sumsq(xg[1, c])
        x_fwd(c).wait_recv()
        acc = acc + mm(xg[2, c], wq(3))
        sq = sq + sumsq(xg[2, c])
        qkv = (acc * lax.rsqrt(sq / d_model + EPS)).astype(BF16).astype(F32)
        ext[rows8(c), :] = qkv

        @pl.when(i == 0)
        def _():
            edge_out[...] = qkv[CR - 8 :, :]
            edge.start()

        return 0

    lax.fori_loop(0, NC, second_half, 0)
    w_xnb.start()
    w_sib.start()

    def conv_chunk(c):
        r0 = pl.multiple_of(c * CR, CR)
        live = (lax.broadcasted_iota(jnp.int32, (CR, HD), 0) + r0) < length
        for p in range(3):
            for h in range(2):
                lanes = slice(h * HD, (h + 1) * HD)
                slab = ext[pl.ds(r0, CR + 8), p * 256 + h * HD : p * 256 + (h + 1) * HD]
                total = jnp.zeros((CR, HD), F32)
                for j in range(CONV):
                    total = total + conv_ref[j, p : p + 1, lanes] * slab[8 - j : 8 - j + CR, :]
                if p == 0:
                    qb[h, pl.ds(r0, CR), :] = unit_rows(total).astype(BF16)
                elif p == 1:
                    kb[h, pl.ds(r0, CR), :] = jnp.where(live, unit_rows(total), 0.0).astype(BF16)
                else:
                    va[h, pl.ds(r0, CR), 0:HD] = jnp.where(live, total, 0.0).astype(BF16)
                    va[h, pl.ds(r0, CR), HD:] = jnp.where(live, 1.0, 0.0).astype(BF16)

    def conv_step(i, _):
        conv_chunk(i + 1)
        return 0

    lax.fori_loop(0, NC - 1, conv_step, 0)
    edge.wait_recv()
    ext[0:8, :] = edge_in[...] * keep
    conv_chunk(0)

    row = lax.broadcasted_iota(jnp.int32, (16, 256), 0)
    for h in range(2):
        head = group[0] * 2 + h
        alpha, eta, theta = rates_ref[0, 0, head], rates_ref[1, 0, head], rates_ref[2, 0, head]
        kh = kb[h]
        a_mat = lax.dot_general(kh, kh, (((0,), (0,)), ((), ())), preferred_element_type=F32)
        b_mat = lax.dot_general(
            kh, va[h, :, 0:HD], (((0,), (0,)), ((), ())), preferred_element_type=F32
        )
        packet[h, 0:HD, 0:HD] = (a_mat * (theta * keep)).astype(BF16)
        packet[h, 0:HD, HD:] = (b_mat * theta).astype(BF16)
        d_hi, d_lo = split2(jnp.full((16, 256), (1.0 - alpha) * keep, F32))
        e_hi, e_lo = split2(jnp.full((16, 256), eta * keep, F32))
        pick = jnp.where(row == 0, d_hi.astype(F32), jnp.where(row == 1, d_lo.astype(F32), 0.0))
        pick = jnp.where(row == 2, e_hi.astype(F32), jnp.where(row == 3, e_lo.astype(F32), pick))
        packet[h, HD : HD + 16, :] = pick.astype(BF16)
    for d in range(1, span):
        state(d).start()

    tri = lax.broadcasted_iota(jnp.int32, (CR, CR), 1) <= lax.broadcasted_iota(jnp.int32, (CR, CR), 0)
    for c in range(NC):
        for h in range(2):
            q8 = qb[h, c * CR : (c + 1) * CR, :] * 8
            pv = mm(jnp.exp(mm_t(q8, pkb[h])).astype(BF16), pva[h])
            if c:
                w = jnp.exp(mm_t(q8, kb[h, 0 : c * CR, :])).astype(BF16)
                pv = pv + mm(w, va[h, 0 : c * CR, :])
            w = jnp.where(tri, jnp.exp(mm_t(q8, kb[h, c * CR : (c + 1) * CR, :])), 0.0)
            pv = pv + mm(w.astype(BF16), va[h, c * CR : (c + 1) * CR, :])
            attn[h, c * CR : (c + 1) * CR, :] = pv[:, :HD] / pv[:, HD:]

    w_xnb.wait_recv()
    w_fwd.start()

    def chain(i, carry):
        d = span - 1 - i
        state(d).wait_recv()
        new = []
        for h in range(2):
            mem, mom = carry[2 * h], carry[2 * h + 1]
            scal = states[d - 1, h, HD : HD + 16, 0:HD].astype(F32)
            dec, eta = scal[0:1] + scal[1:2], scal[2:3] + scal[3:4]
            hi, lo = split2(mem)
            a_mat = states[d - 1, h, 0:HD, 0:HD]
            mom = eta * mom - (mm(a_mat, hi) + mm(a_mat, lo)) + states[d - 1, h, 0:HD, HD:].astype(F32)
            new += [dec * mem + mom, mom]
        return tuple(new)

    zero = jnp.zeros((HD, HD), F32)
    carry = (zero, zero, zero, zero)
    if span <= 4:
        for i in range(span - 1):
            carry = chain(i, carry)
    else:
        carry = lax.fori_loop(0, span - 1, chain, carry)
    mats = [split2(carry[2 * h] * keep) for h in range(2)]

    for c in range(NC):
        for h in range(2):
            qh = qb[h, c * CR : (c + 1) * CR, :]
            retr = mm(qh, mats[h][0]) + mm(qh, mats[h][1])
            mem = retr * lax.rsqrt(jnp.mean(retr * retr, -1, keepdims=True) + EPS)
            hog[0, c, :, h * HD : (h + 1) * HD] = (
                attn[h, c * CR : (c + 1) * CR, :] + mem
            ).astype(BF16)
        h_xnb(c).start()
        h_sib(c).start()

    w_sib.wait_recv()
    w_fwd.wait_recv()

    def wo(s, t):
        return wout_ref[:, cols[t]] if s == 0 else wog[s - 1, :, cols[t]]

    def wrows(ref, t):
        return ref[cols[t], :]

    def reduce_x(c):
        rs1(c).wait_recv()
        rs2_out[c] = (part2[c] + rs1_in[c, 1].astype(F32)).astype(BF16)
        rs2(c).start()
        part0[c] = part0[c] + rs1_in[c, 0].astype(F32)

    def ffn(c, _):
        h_xnb(c).wait_recv()
        h_fwd(c).start()
        h_sib(c).wait_recv()
        h0, h1, h2 = hog[0, c], hog[1, c], hog[2, c]
        accs = [mm(h0, wo(0, t)) + mm(h1, wo(1, t)) + mm(h2, wo(2, t)) for t in range(4)]
        h_fwd(c).wait_recv()
        h3 = hog[3, c]
        res = []
        sq = jnp.zeros((CR, 1), F32)
        for t in range(4):
            xt = x_ref[c] if t == 0 else xg[t - 1, c]
            r = (xt.astype(F32) + (accs[t] + mm(h3, wo(3, t)))).astype(BF16)
            sq = sq + sumsq(r)
            res.append(r)
        resid0[...] = res[0].astype(F32)
        inv = lax.rsqrt(sq / d_model + EPS)

        @pl.when(c > 0)
        def _():
            reduce_x(c - 1)

        gate = sum(mm(res[t], wrows(wgate_ref, t)) for t in range(4)) * inv
        up = sum(mm(res[t], wrows(wup_ref, t)) for t in range(4)) * inv
        hidden = (gate / (1.0 + jnp.exp(-gate)) * up).astype(BF16)
        rs1_out[c, 0] = mm(hidden, wdown_ref[:, cols[1]]).astype(BF16)
        rs1_out[c, 1] = mm(hidden, wdown_ref[:, cols[3]]).astype(BF16)
        rs1(c).start()
        part2[c] = mm(hidden, wdown_ref[:, cols[2]])
        part0[c] = mm(hidden, wdown_ref[:, cols[0]]) + resid0[...]
        return 0

    lax.fori_loop(0, NC, ffn, 0)
    reduce_x(NC - 1)

    def last(c, _):
        rs2(c).wait_recv()
        out_ref[c] = (part0[c] + rs2_in[c].astype(F32)).astype(BF16)
        return 0

    lax.fori_loop(0, NC, last, 0)

    def drain(c, _):
        for copy in (x_sib, x_xnb, x_fwd, h_sib, h_xnb, h_fwd, rs1, rs2):
            copy(c).wait_send()
        return 0

    lax.fori_loop(0, NC, drain, 0)
    w_sib.wait_send()
    w_xnb.wait_send()
    w_fwd.wait_send()
    edge.wait_send()
    for d in range(1, span):
        state(d).wait_send()


def body(n_seq, activations, seg_len, seg_start, memory_rates, w_qkv, conv_w, persistent, w_out, w_gate, w_up, w_down):
    span = n_seq // 2
    full = w_qkv.shape[0]
    hw = w_qkv.shape[2]
    ff = w_gate.shape[1]
    vmem = pl.BlockSpec(memory_space=pltpu.VMEM)
    smem = pl.BlockSpec(memory_space=pltpu.SMEM)
    dma = pltpu.SemaphoreType.DMA
    per_chunk = dma((NC,))
    out = pl.pallas_call(
        functools.partial(kernel, n_seq, span),
        out_shape=jax.ShapeDtypeStruct((NC, CR, hw), BF16),
        in_specs=[smem, smem, smem] + [vmem] * 8,
        out_specs=vmem,
        scratch_shapes=[
            pltpu.VMEM((3, NC, CR, hw), BF16),
            pltpu.VMEM((SEG + 8, 3 * hw), F32),
            pltpu.VMEM((8, 3 * hw), F32),
            pltpu.VMEM((8, 3 * hw), F32),
            pltpu.VMEM((2, SEG, HD), BF16),
            pltpu.VMEM((2, SEG, HD), BF16),
            pltpu.VMEM((2, SEG, 2 * HD), BF16),
            pltpu.VMEM((2, HD, HD), BF16),
            pltpu.VMEM((2, HD, 2 * HD), BF16),
            pltpu.VMEM((2, SEG, HD), F32),
            pltpu.VMEM((2, HD + 16, 2 * HD), BF16),
            pltpu.VMEM((span - 1, 2, HD + 16, 2 * HD), BF16),
            pltpu.VMEM((3, hw, full), BF16),
            pltpu.VMEM((4, NC, CR, hw), BF16),
            pltpu.VMEM((CR, hw), F32),
            pltpu.VMEM((NC, CR, hw), F32),
            pltpu.VMEM((NC, CR, hw), F32),
            pltpu.VMEM((NC, 2, CR, hw), BF16),
            pltpu.VMEM((NC, 2, CR, hw), BF16),
            pltpu.VMEM((NC, CR, hw), BF16),
            pltpu.VMEM((NC, CR, hw), BF16),
        ]
        + [per_chunk] * 6
        + [dma((3,))] * 2
        + [per_chunk] * 6
        + [dma, dma]
        + [dma((span - 1,))] * 2
        + [per_chunk] * 4,
        compiler_params=pltpu.CompilerParams(
            collective_id=0, has_side_effects=True, vmem_limit_bytes=56 * 1024 * 1024
        ),
    )(
        seg_len,
        seg_start,
        memory_rates,
        activations.reshape(NC, CR, hw),
        w_qkv.reshape(full, 3 * hw),
        conv_w,
        persistent,
        w_out,
        w_gate,
        w_up,
        w_down,
    )
    return out.reshape(SEG, hw)


def solution(mesh):
    return jax.shard_map(
        functools.partial(body, mesh.shape["seq"]),
        mesh=mesh,
        in_specs=(
            P("seq", ("tr", "tc")),
            P("seq"),
            P("seq"),
            P(None, "seq", None),
            P(None, None, ("tr", "tc")),
            P(None, None, ("tr", "tc")),
            P(None, None, ("tr", "tc")),
            P(("tr", "tc"), None),
            P(None, ("tr", "tc")),
            P(None, ("tr", "tc")),
            P(("tr", "tc"), None),
        ),
        out_specs=P("seq", ("tr", "tc")),
        check_vma=False,
    )
```

time: 279 us -> 79.1 us (0.28)
  waiting for transfers between devices: 178 us -> 0 us
  Pallas kernels: 0 us -> 68 us
  matrix products: 50.4 us -> 0 us
  other arithmetic: 17.2 us -> 0 us
  between operations: 15.1 us -> 1.33 us
  starting transfers between devices: 3.99 us -> 0 us
  local copies, waits for them, and re-layouts: 13.4 us -> 9.6 us
    all_gather x4 -> x0, waiting for transfers between devices: 114 us -> none  [the longest x2 68.4 us: carried_in(): lax.all_gather(part.astype(kind), axis)]
    pallas_call x0 -> x1, Pallas kernels: none -> 68 us  [body(): pl.pallas_call(functools.partial(kernel, n_seq, span), out_shape=jax.Shap...]
    reduce_scatter x2 -> x0, waiting for transfers between devices: 61.6 us -> none  [the longest x1 31.6 us: body(): lax.psum_scatter(down.astype(jnp.bfloat16), ('tr', 'tc'), scatter_dimensi...]
    dot_general x19 -> x0, matrix products: 50.4 us -> none  [the longest x8 11.2 us: exact_product(): return jnp.matmul(left, right, precision=lax.Precision.HIGHEST)]
    convert_element_type x8 -> x0, other arithmetic: 5.98 us -> none  [the longest x1 1.96 us: body(): resid = (activations.astype(jnp.float32) + share).astype(jnp.bfloat16)]
    unnamed x26 -> x9, local copies, waits for them, and re-layouts: 2.85 us -> 8.02 us
    reduce_sum x5 -> x0, other arithmetic: 4.93 us -> none  [the longest x1 2.07 us: body(): squares = jnp.sum(piece_f * piece_f, -1)]
    add x2 -> x0, other arithmetic: 3.79 us -> none  [the longest x1 3.79 us: body(): convolved + jnp.where(valid[:, None], taps[offset] * shifted, 0.0)]
  transfers between devices with their start and end apart: 7 -> 0, of which waited for: 7 -> 0; matrix products, arithmetic and copies ran while one was open for 9% -> 0% of each run, Pallas kernels for 0% -> 0%
where the time goes in v1:
time: 79.1 us; the launch traced here: 78.9 us
  Pallas kernels  68 us (86%)
  local copies, waits for them, and re-layouts  9.6 us (12%)
  between operations  1.33 us (2%)
    pallas_call x1, Pallas kernels, body(): pl.pallas_call(functools.partial(kernel, n_seq, span), out_shape=jax.Shap...  68 us
    unnamed x9, local copies, waits for them, and re-layouts  8.02 us
    reshape x1, local copies, waits for them, and re-layouts, body(): w_qkv.reshape(full, 3 * hw)  1.59 us

profile of v1, /device:TPU:0, one launch (start us, length us, event | category | flops | bytes accessed | tf_op | source)
XLA Modules:
  0.0 78.9 jit_solution(10302630432793052253)
XLA Ops:
  1.3 1.3 %copy.18.conv_ref = f32[4,3,256]{2,1,0:T(4,128)} copy(f32[4,3,256]{2,0,1:T(4,128)} %param.16) | data formatting | bytes 24576 | tf_op args[5]
  2.6 1.7 %copy.16 = bf16[1024,3,256]{0,2,1:T(8,128)(2,1)S(1)} copy(bf16[1024,3,256]{2,0,1:T(8,128)(2,1)} %param.15) | data formatting | bytes 3145728 | tf_op args[4]
  4.3 0.0 copy-start
  4.3 1.6 %copy.17.wqkv_ref = bf16[1024,768]{1,0:T(8,128)(2,1)} copy(bf16[1024,768]{0,1:T(8,128)(2,1)S(1)} %bitcast.3) | data formatting | bytes 3145728 | tf_op jit(solution)/shard_map/reshape | solution.py:409
  5.9 0.0 copy-done
  5.9 0.0 copy-start.1
  5.9 1.6 %copy.19.wgate_ref = bf16[1024,704]{1,0:T(8,128)(2,1)} copy(bf16[1024,704]{0,1:T(8,128)(2,1)S(1)} %copy-done) | data formatting | bytes 2883584 | tf_op args[8]
  7.5 0.0 copy-done.1
  7.5 1.6 %copy.20.wup_ref = bf16[1024,704]{1,0:T(8,128)(2,1)} copy(bf16[1024,704]{0,1:T(8,128)(2,1)S(1)} %copy-done.1) | data formatting | bytes 2883584 | tf_op args[9]
  9.1 68.0 %shard_map.109 = bf16[4,256,256]{2,1,0:T(8,128)(2,1)} custom-call(s32[1]{0:T(128)S(6)} %copy.22.len_ref, s32[1]{0:T(128)S(6)} %copy.23.start_ref, f32[3,1,8]{2,1,0:T(1,128)} %rates_ref.1, bf16[4,256,256]{2,1,0:T(8,128)(2,1)} %bitcast.5, bf16[1024,768]{1,0:T(8,128)(2,1)} %copy.17.wqkv_ref, f32[4,3,256]{2,1,0:T(4,128)} %copy.18.conv_ref, ...), custom_call_target="tpu_custom_call" | custom-call | tf_op jit(solution)/shard_map/pallas_call | solution.py:367
  77.0 1.9 %copy.24 = bf16[1024,256]{1,0:T(8,128)(2,1)} copy(bf16[1024,256]{1,0:T(8,128)(2,1)} %bitcast.4) | data formatting | bytes 1048576
Async XLA Ops:
  4.3 1.6 %copy-start = (bf16[1024,704]{0,1:T(8,128)(2,1)S(1)}, bf16[1024,704]{0,1:T(8,128)(2,1)}, u32[]{:S(2)}) copy-start(bf16[1024,704]{0,1:T(8,128)(2,1)} %param.19) | copy-start | bytes 4325380
  5.9 1.6 %copy-start.1 = (bf16[1024,704]{0,1:T(8,128)(2,1)S(1)}, bf16[1024,704]{0,1:T(8,128)(2,1)}, u32[]{:S(2)}) copy-start(bf16[1024,704]{0,1:T(8,128)(2,1)} %param.20) | copy-start | bytes 4325380

commit v2 on v1

--- a/solution.py
+++ b/solution.py
@@ -41,16 +41,20 @@
     len_ref,
     start_ref,
     rates_ref,
-    x_ref,
-    wqkv_ref,
+    x_hbm,
+    wqkv_hbm,
     conv_ref,
     pers_ref,
-    wout_ref,
+    wout_hbm,
+    wgate_hbm,
+    wup_hbm,
+    wdown_hbm,
+    out_ref,
+    xg,
+    wqkv_ref,
     wgate_ref,
     wup_ref,
     wdown_ref,
-    out_ref,
-    xg,
     ext,
     edge_out,
     edge_in,
@@ -60,6 +64,7 @@
     pkb,
     pva,
     attn,
+    ab,
     packet,
     states,
     wog,
@@ -77,6 +82,7 @@
     ed_s, ed_r,
     st_s, st_r,
     r1_s, r1_r, r2_s, r2_r,
+    lc_s,
 ):
     seq, tr, tc = lax.axis_index("seq"), lax.axis_index("tr"), lax.axis_index("tc")
     sib = (seq, tr, 1 - tc)
@@ -93,6 +99,22 @@
             src_ref=src, dst_ref=dst, send_sem=ssem, recv_sem=rsem, device_id=dev, device_id_type=MESH
         )
 
+    fetches = [
+        pltpu.make_async_copy(src, dst, lc_s.at[i])
+        for i, (src, dst) in enumerate(
+            (
+                (x_hbm, xg.at[0]),
+                (wqkv_hbm, wqkv_ref),
+                (wout_hbm, wog.at[0]),
+                (wgate_hbm, wgate_ref),
+                (wup_hbm, wup_ref),
+                (wdown_hbm, wdown_ref),
+            )
+        )
+    ]
+    for fetch in fetches:
+        fetch.start()
+
     barrier = pltpu.get_barrier_semaphore()
     peers = [sib, xnb] + [ahead(d) for d in range(1, span)] + [ahead(n_seq - d) for d in range(1, span)]
     for peer in peers:
@@ -100,13 +122,13 @@
     pl.semaphore_wait(barrier, len(peers))
 
     def x_sib(c):
-        return send(x_ref.at[c], xg.at[0, c], xs_s.at[c], xs_r.at[c], sib)
+        return send(x_hbm.at[c], xg.at[1, c], xs_s.at[c], xs_r.at[c], sib)
 
     def x_xnb(c):
-        return send(x_ref.at[c], xg.at[1, c], xx_s.at[c], xx_r.at[c], xnb)
+        return send(x_hbm.at[c], xg.at[2, c], xx_s.at[c], xx_r.at[c], xnb)
 
     def x_fwd(c):
-        return send(xg.at[1, c], xg.at[2, c], xf_s.at[c], xf_r.at[c], sib)
+        return send(xg.at[2, c], xg.at[3, c], xf_s.at[c], xf_r.at[c], sib)
 
     def h_sib(c):
         return send(hog.at[0, c], hog.at[1, c], hs_s.at[c], hs_r.at[c], sib)
@@ -123,9 +145,9 @@
     def rs2(c):
         return send(rs2_out.at[c], rs2_in.at[c], r2_s.at[c], r2_r.at[c], xnb)
 
-    w_sib = send(wout_ref, wog.at[0], ws_s.at[0], ws_r.at[0], sib)
-    w_xnb = send(wout_ref, wog.at[1], ws_s.at[1], ws_r.at[1], xnb)
-    w_fwd = send(wog.at[1], wog.at[2], ws_s.at[2], ws_r.at[2], sib)
+    w_sib = send(wog.at[0], wog.at[1], ws_s.at[0], ws_r.at[0], sib)
+    w_xnb = send(wog.at[0], wog.at[2], ws_s.at[1], ws_r.at[1], xnb)
+    w_fwd = send(wog.at[2], wog.at[3], ws_s.at[2], ws_r.at[2], sib)
     edge = send(edge_out, edge_in, ed_s, ed_r, ahead(1))
 
     def state(d):
@@ -148,91 +170,87 @@
         pva[h, 0:16, 0:HD] = pers_ref[1, :, lanes]
         pva[h, 0:16, HD:] = jnp.ones((16, HD), BF16)
 
-    def wq(t):
-        return wqkv_ref[pl.ds(pl.multiple_of(group[t] * 256, 256), 256), :]
+    def project(c, pair):
+        lhs = [xg[t, c] for t in pair]
+        return [
+            sum(mm(x, wqkv_ref[p, cols[t], :]) for x, t in zip(lhs, pair)) for p in range(3)
+        ]
 
     def rows8(c):
-        return pl.ds(pl.multiple_of(8 + c * CR, 8), CR)
-
-    def first_half(i, _):
-        c = lax.rem(i + NC - 1, NC)
+        return slice(8 + c * CR, 8 + (c + 1) * CR)
+
+    fetches[0].wait()
+    fetches[1].wait()
+    for c in order:
         x_sib(c).wait_recv()
-        ext[rows8(c), :] = mm(x_ref[c], wq(0)) + mm(xg[0, c], wq(1))
-        return 0
-
-    lax.fori_loop(0, NC, first_half, 0)
+        for p, part in enumerate(project(c, (0, 1))):
+            ext[rows8(c), p * 256 : (p + 1) * 256] = part
 
     def sumsq(v):
         v = v.astype(F32)
         return jnp.sum(v * v, -1, keepdims=True)
 
-    def second_half(i, _):
-        c = lax.rem(i + NC - 1, NC)
+    def finish_projection(c):
         x_xnb(c).wait_recv()
         x_fwd(c).start()
-        acc = ext[rows8(c), :] + mm(xg[1, c], wq(2))
-        sq = sumsq(x_ref[c]) + sumsq(xg[0, c]) + sumsq(xg[1, c])
+        sq = sumsq(xg[0, c]) + sumsq(xg[1, c]) + sumsq(xg[2, c])
         x_fwd(c).wait_recv()
-        acc = acc + mm(xg[2, c], wq(3))
-        sq = sq + sumsq(xg[2, c])
-        qkv = (acc * lax.rsqrt(sq / d_model + EPS)).astype(BF16).astype(F32)
-        ext[rows8(c), :] = qkv
-
-        @pl.when(i == 0)
-        def _():
-            edge_out[...] = qkv[CR - 8 :, :]
-            edge.start()
-
-        return 0
-
-    lax.fori_loop(0, NC, second_half, 0)
-    w_xnb.start()
-    w_sib.start()
+        inv = lax.rsqrt((sq + sumsq(xg[3, c])) / d_model + EPS)
+        for p, part in enumerate(project(c, (2, 3))):
+            lanes = slice(p * 256, (p + 1) * 256)
+            ext[rows8(c), lanes] = ((ext[rows8(c), lanes] + part) * inv).astype(BF16).astype(F32)
 
     def conv_chunk(c):
-        r0 = pl.multiple_of(c * CR, CR)
-        live = (lax.broadcasted_iota(jnp.int32, (CR, HD), 0) + r0) < length
+        rows = slice(c * CR, (c + 1) * CR)
+        live = (lax.broadcasted_iota(jnp.int32, (CR, HD), 0) + c * CR) < length
         for p in range(3):
             for h in range(2):
                 lanes = slice(h * HD, (h + 1) * HD)
-                slab = ext[pl.ds(r0, CR + 8), p * 256 + h * HD : p * 256 + (h + 1) * HD]
+                slab = ext[c * CR : (c + 1) * CR + 8, p * 256 + h * HD : p * 256 + (h + 1) * HD]
                 total = jnp.zeros((CR, HD), F32)
                 for j in range(CONV):
-                    total = total + conv_ref[j, p : p + 1, lanes] * slab[8 - j : 8 - j + CR, :]
+                    total = total + conv_ref[p, j : j + 1, lanes] * slab[8 - j : 8 - j + CR, :]
                 if p == 0:
-                    qb[h, pl.ds(r0, CR), :] = unit_rows(total).astype(BF16)
+                    qb[h, rows, :] = unit_rows(total).astype(BF16)
                 elif p == 1:
-                    kb[h, pl.ds(r0, CR), :] = jnp.where(live, unit_rows(total), 0.0).astype(BF16)
+                    kb[h, rows, :] = jnp.where(live, unit_rows(total), 0.0).astype(BF16)
                 else:
-                    va[h, pl.ds(r0, CR), 0:HD] = jnp.where(live, total, 0.0).astype(BF16)
-                    va[h, pl.ds(r0, CR), HD:] = jnp.where(live, 1.0, 0.0).astype(BF16)
-
-    def conv_step(i, _):
-        conv_chunk(i + 1)
-        return 0
-
-    lax.fori_loop(0, NC - 1, conv_step, 0)
+                    va[h, rows, 0:HD] = jnp.where(live, total, 0.0).astype(BF16)
+                    va[h, rows, HD:] = jnp.where(live, 1.0, 0.0).astype(BF16)
+        for h in range(2):
+            kh = kb[h, rows, :]
+            both = jnp.concatenate([kh, va[h, rows, 0:HD]], 1)
+            term = lax.dot_general(kh, both, (((0,), (0,)), ((), ())), preferred_element_type=F32)
+            ab[h] = term if c == 0 else ab[h] + term
+
+    finish_projection(NC - 1)
+    edge_out[...] = ext[SEG : SEG + 8, :]
+    edge.start()
+    finish_projection(0)
     edge.wait_recv()
     ext[0:8, :] = edge_in[...] * keep
     conv_chunk(0)
+    for c in range(1, NC - 1):
+        finish_projection(c)
+        if c == NC - 2:
+            fetches[2].wait()
+            w_xnb.start()
+            w_sib.start()
+        conv_chunk(c)
+    conv_chunk(NC - 1)
 
     row = lax.broadcasted_iota(jnp.int32, (16, 256), 0)
     for h in range(2):
         head = group[0] * 2 + h
         alpha, eta, theta = rates_ref[0, 0, head], rates_ref[1, 0, head], rates_ref[2, 0, head]
-        kh = kb[h]
-        a_mat = lax.dot_general(kh, kh, (((0,), (0,)), ((), ())), preferred_element_type=F32)
-        b_mat = lax.dot_general(
-            kh, va[h, :, 0:HD], (((0,), (0,)), ((), ())), preferred_element_type=F32
-        )
-        packet[h, 0:HD, 0:HD] = (a_mat * (theta * keep)).astype(BF16)
-        packet[h, 0:HD, HD:] = (b_mat * theta).astype(BF16)
+        packet[h, 0:HD, 0:HD] = (ab[h, :, 0:HD] * (theta * keep)).astype(BF16)
+        packet[h, 0:HD, HD:] = (ab[h, :, HD:] * theta).astype(BF16)
         d_hi, d_lo = split2(jnp.full((16, 256), (1.0 - alpha) * keep, F32))
         e_hi, e_lo = split2(jnp.full((16, 256), eta * keep, F32))
         pick = jnp.where(row == 0, d_hi.astype(F32), jnp.where(row == 1, d_lo.astype(F32), 0.0))
         pick = jnp.where(row == 2, e_hi.astype(F32), jnp.where(row == 3, e_lo.astype(F32), pick))
         packet[h, HD : HD + 16, :] = pick.astype(BF16)
-    for d in range(1, span):
+    for d in range(span - 1, 0, -1):
         state(d).start()
 
     tri = lax.broadcasted_iota(jnp.int32, (CR, CR), 1) <= lax.broadcasted_iota(jnp.int32, (CR, CR), 0)
@@ -286,12 +304,14 @@
 
     w_sib.wait_recv()
     w_fwd.wait_recv()
+    for fetch in fetches[3:]:
+        fetch.wait()
 
     def wo(s, t):
-        return wout_ref[:, cols[t]] if s == 0 else wog[s - 1, :, cols[t]]
+        return wog[s, :, cols[t]]
 
     def wrows(ref, t):
-        return ref[cols[t], :]
+        return ref[:, cols[t]]
 
     def reduce_x(c):
         rs1(c).wait_recv()
@@ -310,8 +330,7 @@
         res = []
         sq = jnp.zeros((CR, 1), F32)
         for t in range(4):
-            xt = x_ref[c] if t == 0 else xg[t - 1, c]
-            r = (xt.astype(F32) + (accs[t] + mm(h3, wo(3, t)))).astype(BF16)
+            r = (xg[t, c].astype(F32) + (accs[t] + mm(h3, wo(3, t)))).astype(BF16)
             sq = sq + sumsq(r)
             res.append(r)
         resid0[...] = res[0].astype(F32)
@@ -321,8 +340,8 @@
         def _():
             reduce_x(c - 1)
 
-        gate = sum(mm(res[t], wrows(wgate_ref, t)) for t in range(4)) * inv
-        up = sum(mm(res[t], wrows(wup_ref, t)) for t in range(4)) * inv
+        gate = sum(mm_t(res[t], wrows(wgate_ref, t)) for t in range(4)) * inv
+        up = sum(mm_t(res[t], wrows(wup_ref, t)) for t in range(4)) * inv
         hidden = (gate / (1.0 + jnp.exp(-gate)) * up).astype(BF16)
         rs1_out[c, 0] = mm(hidden, wdown_ref[:, cols[1]]).astype(BF16)
         rs1_out[c, 1] = mm(hidden, wdown_ref[:, cols[3]]).astype(BF16)
@@ -361,16 +380,21 @@
     hw = w_qkv.shape[2]
     ff = w_gate.shape[1]
     vmem = pl.BlockSpec(memory_space=pltpu.VMEM)
+    hbm = pl.BlockSpec(memory_space=pl.ANY)
     smem = pl.BlockSpec(memory_space=pltpu.SMEM)
     dma = pltpu.SemaphoreType.DMA
     per_chunk = dma((NC,))
     out = pl.pallas_call(
         functools.partial(kernel, n_seq, span),
         out_shape=jax.ShapeDtypeStruct((NC, CR, hw), BF16),
-        in_specs=[smem, smem, smem] + [vmem] * 8,
+        in_specs=[smem, smem, smem, hbm, hbm, vmem, vmem] + [hbm] * 4,
         out_specs=vmem,
         scratch_shapes=[
-            pltpu.VMEM((3, NC, CR, hw), BF16),
+            pltpu.VMEM((4, NC, CR, hw), BF16),
+            pltpu.VMEM((3, full, hw), BF16),
+            pltpu.VMEM((ff, full), BF16),
+            pltpu.VMEM((ff, full), BF16),
+            pltpu.VMEM((ff, full), BF16),
             pltpu.VMEM((SEG + 8, 3 * hw), F32),
             pltpu.VMEM((8, 3 * hw), F32),
             pltpu.VMEM((8, 3 * hw), F32),
@@ -380,9 +404,10 @@
             pltpu.VMEM((2, HD, HD), BF16),
             pltpu.VMEM((2, HD, 2 * HD), BF16),
             pltpu.VMEM((2, SEG, HD), F32),
+            pltpu.VMEM((2, HD, 2 * HD), F32),
             pltpu.VMEM((2, HD + 16, 2 * HD), BF16),
             pltpu.VMEM((span - 1, 2, HD + 16, 2 * HD), BF16),
-            pltpu.VMEM((3, hw, full), BF16),
+            pltpu.VMEM((4, hw, full), BF16),
             pltpu.VMEM((4, NC, CR, hw), BF16),
             pltpu.VMEM((CR, hw), F32),
             pltpu.VMEM((NC, CR, hw), F32),
@@ -397,7 +422,8 @@
         + [per_chunk] * 6
         + [dma, dma]
         + [dma((span - 1,))] * 2
-        + [per_chunk] * 4,
+        + [per_chunk] * 4
+        + [dma((6,))],
         compiler_params=pltpu.CompilerParams(
             collective_id=0, has_side_effects=True, vmem_limit_bytes=56 * 1024 * 1024
         ),
@@ -406,12 +432,12 @@
         seg_start,
         memory_rates,
         activations.reshape(NC, CR, hw),
-        w_qkv.reshape(full, 3 * hw),
-        conv_w,
+        jnp.transpose(w_qkv, (1, 0, 2)),
+        jnp.transpose(conv_w, (1, 0, 2)),
         persistent,
         w_out,
-        w_gate,
-        w_up,
+        w_gate.T,
+        w_up.T,
         w_down,
     )
     return out.reshape(SEG, hw)

time: 79.1 us -> 68.3 us (0.86)
  local copies, waits for them, and re-layouts: 9.6 us -> 1.87 us
  Pallas kernels: 68 us -> 64.8 us
    unnamed x9 -> x1, local copies, waits for them, and re-layouts: 8.02 us -> 1.87 us
    pallas_call x1, Pallas kernels: 68 us -> 64.8 us  [body(): pl.pallas_call(functools.partial(kernel, n_seq, span), out_shape=jax.Shap...]
    reshape x1 -> x0, local copies, waits for them, and re-layouts: 1.59 us -> none  [body(): w_qkv.reshape(full, 3 * hw)]
where the time goes in v2:
time: 68.3 us; the launch traced here: 68 us
  Pallas kernels  64.8 us (95%)
  local copies, waits for them, and re-layouts  1.87 us (3%)
  between operations  1.3 us (2%)
    pallas_call x1, Pallas kernels, body(): pl.pallas_call(functools.partial(kernel, n_seq, span), out_shape=jax.Shap...  64.8 us
    unnamed x1, local copies, waits for them, and re-layouts  1.87 us

profile of v2, /device:TPU:0, one launch (start us, length us, event | category | flops | bytes accessed | tf_op | source)
XLA Modules:
  0.0 68.0 jit_solution(5854956803413133825)
XLA Ops:
  1.3 64.8 %shard_map.109 = bf16[4,256,256]{2,1,0:T(8,128)(2,1)} custom-call(s32[1]{0:T(128)S(6)} %copy.13.len_ref, s32[1]{0:T(128)S(6)} %copy.14.start_ref, f32[3,1,8]{2,1,0:T(1,128)} %rates_ref.1, bf16[4,256,256]{2,1,0:T(8,128)(2,1)} %bitcast.10, bf16[3,1024,256]{2,1,0:T(8,128)(2,1)} %bitcast.7, f32[3,4,256]{2,1,0:T(4,128)} %bitcast.11, ...), custom_call_target="tpu_custom_call" | custom-call | tf_op jit(solution)/shard_map/pallas_call | solution.py:387
  66.1 1.9 %copy.15 = bf16[1024,256]{1,0:T(8,128)(2,1)} copy(bf16[1024,256]{1,0:T(8,128)(2,1)} %bitcast.6) | data formatting | bytes 1048576

commit v3 on v2

--- a/solution.py
+++ b/solution.py
@@ -65,11 +65,16 @@
     pva,
     attn,
     ab,
-    packet,
-    states,
+    pk_a,
+    pk_b,
+    st_a,
+    st_b,
+    mid_out,
+    mid_in,
+    projb,
+    resb,
     wog,
     hog,
-    resid0,
     part0,
     part2,
     rs1_out,
@@ -80,7 +85,9 @@
     ws_s, ws_r,
     hs_s, hs_r, hx_s, hx_r, hf_s, hf_r,
     ed_s, ed_r,
-    st_s, st_r,
+    sa_s, sa_r,
+    sb_s, sb_r,
+    md_s, md_r,
     r1_s, r1_r, r2_s, r2_r,
     lc_s,
 ):
@@ -115,8 +122,11 @@
     for fetch in fetches:
         fetch.start()
 
+    short = span == 4
+    reach = 3 if short else span
+    direct = 2 if short else span
     barrier = pltpu.get_barrier_semaphore()
-    peers = [sib, xnb] + [ahead(d) for d in range(1, span)] + [ahead(n_seq - d) for d in range(1, span)]
+    peers = [sib, xnb] + [ahead(d) for d in range(1, reach)] + [ahead(n_seq - d) for d in range(1, reach)]
     for peer in peers:
         pl.semaphore_signal(barrier, inc=1, device_id=peer, device_id_type=MESH)
     pl.semaphore_wait(barrier, len(peers))
@@ -150,8 +160,13 @@
     w_fwd = send(wog.at[2], wog.at[3], ws_s.at[2], ws_r.at[2], sib)
     edge = send(edge_out, edge_in, ed_s, ed_r, ahead(1))
 
-    def state(d):
-        return send(packet, states.at[d - 1], st_s.at[d - 1], st_r.at[d - 1], ahead(d))
+    def map_a(d):
+        return send(pk_a, st_a.at[d - 1], sa_s.at[d - 1], sa_r.at[d - 1], ahead(d))
+
+    def map_b(d):
+        return send(pk_b, st_b.at[d - 1], sb_s.at[d - 1], sb_r.at[d - 1], ahead(d))
+
+    middle = send(mid_out, mid_in, md_s, md_r, ahead(2)) if short else None
 
     order = (NC - 1,) + tuple(range(NC - 1))
     for c in order:
@@ -239,22 +254,34 @@
         conv_chunk(c)
     conv_chunk(NC - 1)
 
-    row = lax.broadcasted_iota(jnp.int32, (16, 256), 0)
+    row = lax.broadcasted_iota(jnp.int32, (16, HD), 0)
+    rates = [[rates_ref[k, 0, group[0] * 2 + h] for k in range(3)] for h in range(2)]
     for h in range(2):
-        head = group[0] * 2 + h
-        alpha, eta, theta = rates_ref[0, 0, head], rates_ref[1, 0, head], rates_ref[2, 0, head]
-        packet[h, 0:HD, 0:HD] = (ab[h, :, 0:HD] * (theta * keep)).astype(BF16)
-        packet[h, 0:HD, HD:] = (ab[h, :, HD:] * theta).astype(BF16)
-        d_hi, d_lo = split2(jnp.full((16, 256), (1.0 - alpha) * keep, F32))
-        e_hi, e_lo = split2(jnp.full((16, 256), eta * keep, F32))
+        pk_b[h] = (ab[h, :, HD:] * rates[h][2]).astype(BF16)
+    for d in range(direct - 1, 0, -1):
+        map_b(d).start()
+    for h in range(2):
+        alpha, eta, theta = rates[h]
+        pk_a[h, 0:HD, :] = (ab[h, :, 0:HD] * (theta * keep)).astype(BF16)
+        d_hi, d_lo = split2(jnp.full((16, HD), (1.0 - alpha) * keep, F32))
+        e_hi, e_lo = split2(jnp.full((16, HD), eta * keep, F32))
         pick = jnp.where(row == 0, d_hi.astype(F32), jnp.where(row == 1, d_lo.astype(F32), 0.0))
         pick = jnp.where(row == 2, e_hi.astype(F32), jnp.where(row == 3, e_lo.astype(F32), pick))
-        packet[h, HD : HD + 16, :] = pick.astype(BF16)
-    for d in range(span - 1, 0, -1):
-        state(d).start()
+        pk_a[h, HD : HD + 16, :] = pick.astype(BF16)
+    for d in range(direct - 1, 0, -1):
+        map_a(d).start()
+
+    def advance(mem, mom, a_ref, b_ref, h):
+        scal = a_ref[h, HD : HD + 16, :].astype(F32)
+        dec, eta = scal[0:1] + scal[1:2], scal[2:3] + scal[3:4]
+        hi, lo = split2(mem)
+        a_mat = a_ref[h, 0:HD, :]
+        mom = eta * mom - (mm(a_mat, hi) + mm(a_mat, lo)) + b_ref[h].astype(F32)
+        return dec * mem + mom, mom
 
     tri = lax.broadcasted_iota(jnp.int32, (CR, CR), 1) <= lax.broadcasted_iota(jnp.int32, (CR, CR), 0)
-    for c in range(NC):
+
+    def attend(c):
         for h in range(2):
             q8 = qb[h, c * CR : (c + 1) * CR, :] * 8
             pv = mm(jnp.exp(mm_t(q8, pkb[h])).astype(BF16), pva[h])
@@ -265,30 +292,42 @@
             pv = pv + mm(w.astype(BF16), va[h, c * CR : (c + 1) * CR, :])
             attn[h, c * CR : (c + 1) * CR, :] = pv[:, :HD] / pv[:, HD:]
 
+    attend(3)
+    attend(2)
+    if short:
+        map_b(1).wait_recv()
+        for h in range(2):
+            first = st_b[0, h].astype(F32)
+            mem, mom = advance(first, first, pk_a, pk_b, h)
+            mid_out[h, 0] = mem.astype(BF16)
+            mid_out[h, 1] = mom.astype(BF16)
+        middle.start()
+    attend(1)
+    attend(0)
+
     w_xnb.wait_recv()
     w_fwd.start()
 
-    def chain(i, carry):
-        d = span - 1 - i
-        state(d).wait_recv()
-        new = []
+    if short:
+        map_a(1).wait_recv()
+        middle.wait_recv()
+        carry = []
         for h in range(2):
-            mem, mom = carry[2 * h], carry[2 * h + 1]
-            scal = states[d - 1, h, HD : HD + 16, 0:HD].astype(F32)
-            dec, eta = scal[0:1] + scal[1:2], scal[2:3] + scal[3:4]
-            hi, lo = split2(mem)
-            a_mat = states[d - 1, h, 0:HD, 0:HD]
-            mom = eta * mom - (mm(a_mat, hi) + mm(a_mat, lo)) + states[d - 1, h, 0:HD, HD:].astype(F32)
-            new += [dec * mem + mom, mom]
-        return tuple(new)
-
-    zero = jnp.zeros((HD, HD), F32)
-    carry = (zero, zero, zero, zero)
-    if span <= 4:
-        for i in range(span - 1):
-            carry = chain(i, carry)
+            carry += advance(
+                mid_in[h, 0].astype(F32), mid_in[h, 1].astype(F32), st_a.at[0], st_b.at[0], h
+            )
     else:
-        carry = lax.fori_loop(0, span - 1, chain, carry)
+
+        def chain(i, carry):
+            d = span - 1 - i
+            map_b(d).wait_recv()
+            map_a(d).wait_recv()
+            new = []
+            for h in range(2):
+                new += advance(carry[2 * h], carry[2 * h + 1], st_a.at[d - 1], st_b.at[d - 1], h)
+            return tuple(new)
+
+        carry = lax.fori_loop(0, span - 1, chain, (jnp.zeros((HD, HD), F32),) * 4)
     mats = [split2(carry[2 * h] * keep) for h in range(2)]
 
     for c in range(NC):
@@ -307,12 +346,6 @@
     for fetch in fetches[3:]:
         fetch.wait()
 
-    def wo(s, t):
-        return wog[s, :, cols[t]]
-
-    def wrows(ref, t):
-        return ref[:, cols[t]]
-
     def reduce_x(c):
         rs1(c).wait_recv()
         rs2_out[c] = (part2[c] + rs1_in[c, 1].astype(F32)).astype(BF16)
@@ -323,31 +356,30 @@
         h_xnb(c).wait_recv()
         h_fwd(c).start()
         h_sib(c).wait_recv()
-        h0, h1, h2 = hog[0, c], hog[1, c], hog[2, c]
-        accs = [mm(h0, wo(0, t)) + mm(h1, wo(1, t)) + mm(h2, wo(2, t)) for t in range(4)]
+        lhs = jnp.concatenate([hog[0, c], hog[1, c], hog[2, c]], 1)
+        proj = mm(lhs, wog[0:3].reshape(3 * 256, d_model))
         h_fwd(c).wait_recv()
-        h3 = hog[3, c]
-        res = []
+        projb[...] = proj + mm(hog[3, c], wog[3])
         sq = jnp.zeros((CR, 1), F32)
         for t in range(4):
-            r = (xg[t, c].astype(F32) + (accs[t] + mm(h3, wo(3, t)))).astype(BF16)
+            r = (xg[t, c].astype(F32) + projb[:, cols[t]]).astype(BF16)
             sq = sq + sumsq(r)
-            res.append(r)
-        resid0[...] = res[0].astype(F32)
+            resb[:, cols[t]] = r
         inv = lax.rsqrt(sq / d_model + EPS)
 
         @pl.when(c > 0)
         def _():
             reduce_x(c - 1)
 
-        gate = sum(mm_t(res[t], wrows(wgate_ref, t)) for t in range(4)) * inv
-        up = sum(mm_t(res[t], wrows(wup_ref, t)) for t in range(4)) * inv
+        res = resb[...]
+        gate = mm_t(res, wgate_ref[...]) * inv
+        up = mm_t(res, wup_ref[...]) * inv
         hidden = (gate / (1.0 + jnp.exp(-gate)) * up).astype(BF16)
         rs1_out[c, 0] = mm(hidden, wdown_ref[:, cols[1]]).astype(BF16)
         rs1_out[c, 1] = mm(hidden, wdown_ref[:, cols[3]]).astype(BF16)
         rs1(c).start()
         part2[c] = mm(hidden, wdown_ref[:, cols[2]])
-        part0[c] = mm(hidden, wdown_ref[:, cols[0]]) + resid0[...]
+        part0[c] = mm(hidden, wdown_ref[:, cols[0]]) + resb[:, cols[0]].astype(F32)
         return 0
 
     lax.fori_loop(0, NC, ffn, 0)
@@ -370,8 +402,11 @@
     w_xnb.wait_send()
     w_fwd.wait_send()
     edge.wait_send()
-    for d in range(1, span):
-        state(d).wait_send()
+    for d in range(1, direct):
+        map_a(d).wait_send()
+        map_b(d).wait_send()
+    if short:
+        middle.wait_send()
 
 
 def body(n_seq, activations, seg_len, seg_start, memory_rates, w_qkv, conv_w, persistent, w_out, w_gate, w_up, w_down):
@@ -405,11 +440,16 @@
             pltpu.VMEM((2, HD, 2 * HD), BF16),
             pltpu.VMEM((2, SEG, HD), F32),
             pltpu.VMEM((2, HD, 2 * HD), F32),
-            pltpu.VMEM((2, HD + 16, 2 * HD), BF16),
-            pltpu.VMEM((span - 1, 2, HD + 16, 2 * HD), BF16),
+            pltpu.VMEM((2, HD + 16, HD), BF16),
+            pltpu.VMEM((2, HD, HD), BF16),
+            pltpu.VMEM((span - 1, 2, HD + 16, HD), BF16),
+            pltpu.VMEM((span - 1, 2, HD, HD), BF16),
+            pltpu.VMEM((2, 2, HD, HD), BF16),
+            pltpu.VMEM((2, 2, HD, HD), BF16),
+            pltpu.VMEM((CR, full), F32),
+            pltpu.VMEM((CR, full), BF16),
             pltpu.VMEM((4, hw, full), BF16),
             pltpu.VMEM((4, NC, CR, hw), BF16),
-            pltpu.VMEM((CR, hw), F32),
             pltpu.VMEM((NC, CR, hw), F32),
             pltpu.VMEM((NC, CR, hw), F32),
             pltpu.VMEM((NC, 2, CR, hw), BF16),
@@ -421,7 +461,8 @@
         + [dma((3,))] * 2
         + [per_chunk] * 6
         + [dma, dma]
-        + [dma((span - 1,))] * 2
+        + [dma((span - 1,))] * 4
+        + [dma, dma]
         + [per_chunk] * 4
         + [dma((6,))],
         compiler_params=pltpu.CompilerParams(

time: 68.3 us -> 65.9 us (0.965)
  Pallas kernels: 64.8 us -> 62.5 us
    pallas_call x1, Pallas kernels: 64.8 us -> 62.5 us  [body(): pl.pallas_call(functools.partial(kernel, n_seq, span), out_shape=jax.Shap...]
where the time goes in v3:
time: 65.9 us; the launch traced here: 65.7 us
  Pallas kernels  62.5 us (95%)
  local copies, waits for them, and re-layouts  1.87 us (3%)
  between operations  1.3 us (2%)
    pallas_call x1, Pallas kernels, body(): pl.pallas_call(functools.partial(kernel, n_seq, span), out_shape=jax.Shap...  62.5 us
    unnamed x1, local copies, waits for them, and re-layouts  1.87 us

profile of v3, /device:TPU:0, one launch (start us, length us, event | category | flops | bytes accessed | tf_op | source)
XLA Modules:
  0.0 65.7 jit_solution(14260464745016150906)
XLA Ops:
  1.3 62.5 %shard_map.109 = bf16[4,256,256]{2,1,0:T(8,128)(2,1)} custom-call(s32[1]{0:T(128)S(6)} %copy.13.len_ref, s32[1]{0:T(128)S(6)} %copy.14.start_ref, f32[3,1,8]{2,1,0:T(1,128)} %rates_ref.1, bf16[4,256,256]{2,1,0:T(8,128)(2,1)} %bitcast.10, bf16[3,1024,256]{2,1,0:T(8,128)(2,1)} %bitcast.7, f32[3,4,256]{2,1,0:T(4,128)} %bitcast.11, ...), custom_call_target="tpu_custom_call" | custom-call | tf_op jit(solution)/shard_map/pallas_call | solution.py:422
  63.8 1.9 %copy.15 = bf16[1024,256]{1,0:T(8,128)(2,1)} copy(bf16[1024,256]{1,0:T(8,128)(2,1)} %bitcast.6) | data formatting | bytes 1048576

commit v4 on v3

--- a/solution.py
+++ b/solution.py
@@ -156,7 +156,10 @@
         return send(rs2_out.at[c], rs2_in.at[c], r2_s.at[c], r2_r.at[c], xnb)
 
     w_sib = send(wog.at[0], wog.at[1], ws_s.at[0], ws_r.at[0], sib)
-    w_xnb = send(wog.at[0], wog.at[2], ws_s.at[1], ws_r.at[1], xnb)
+    half = pl.ds(pl.multiple_of(lax.rem(seq, 2) * 128, 128), 128)
+    pair = (seq + 1 - 2 * lax.rem(seq, 2), tr, tc)
+    w_xnb = send(wog.at[0, half], wog.at[2, half], ws_s.at[1], ws_r.at[1], xnb)
+    w_pair = send(wog.at[2, half], wog.at[2, half], ws_s.at[3], ws_r.at[3], pair)
     w_fwd = send(wog.at[2], wog.at[3], ws_s.at[2], ws_r.at[2], sib)
     edge = send(edge_out, edge_in, ed_s, ed_r, ahead(1))
 
@@ -302,11 +305,11 @@
             mid_out[h, 0] = mem.astype(BF16)
             mid_out[h, 1] = mom.astype(BF16)
         middle.start()
+    w_xnb.wait_recv()
+    w_pair.start()
     attend(1)
     attend(0)
 
-    w_xnb.wait_recv()
-    w_fwd.start()
 
     if short:
         map_a(1).wait_recv()
@@ -341,6 +344,8 @@
         h_xnb(c).start()
         h_sib(c).start()
 
+    w_pair.wait_recv()
+    w_fwd.start()
     w_sib.wait_recv()
     w_fwd.wait_recv()
     for fetch in fetches[3:]:
@@ -401,6 +406,7 @@
     w_sib.wait_send()
     w_xnb.wait_send()
     w_fwd.wait_send()
+    w_pair.wait_send()
     edge.wait_send()
     for d in range(1, direct):
         map_a(d).wait_send()
@@ -458,7 +464,7 @@
             pltpu.VMEM((NC, CR, hw), BF16),
         ]
         + [per_chunk] * 6
-        + [dma((3,))] * 2
+        + [dma((4,))] * 2
         + [per_chunk] * 6
         + [dma, dma]
         + [dma((span - 1,))] * 4

time: 65.9 us -> 64 us (0.971)
  Pallas kernels: 62.5 us -> 60.5 us
    pallas_call x1, Pallas kernels: 62.5 us -> 60.5 us  [body(): pl.pallas_call(functools.partial(kernel, n_seq, span), out_shape=jax.Shap...]
where the time goes in v4:
time: 64 us; the launch traced here: 63.7 us
  Pallas kernels  60.5 us (95%)
  local copies, waits for them, and re-layouts  1.87 us (3%)
  between operations  1.3 us (2%)
    pallas_call x1, Pallas kernels, body(): pl.pallas_call(functools.partial(kernel, n_seq, span), out_shape=jax.Shap...  60.5 us
    unnamed x1, local copies, waits for them, and re-layouts  1.87 us

profile of v4, /device:TPU:0, one launch (start us, length us, event | category | flops | bytes accessed | tf_op | source)
XLA Modules:
  0.0 63.7 jit_solution(1525925796443528317)
XLA Ops:
  1.3 60.5 %shard_map.109 = bf16[4,256,256]{2,1,0:T(8,128)(2,1)} custom-call(s32[1]{0:T(128)S(6)} %copy.13.len_ref, s32[1]{0:T(128)S(6)} %copy.14.start_ref, f32[3,1,8]{2,1,0:T(1,128)} %rates_ref.1, bf16[4,256,256]{2,1,0:T(8,128)(2,1)} %bitcast.10, bf16[3,1024,256]{2,1,0:T(8,128)(2,1)} %bitcast.7, f32[3,4,256]{2,1,0:T(4,128)} %bitcast.11, ...), custom_call_target="tpu_custom_call" | custom-call | tf_op jit(solution)/shard_map/pallas_call | solution.py:428
  61.8 1.9 %copy.15 = bf16[1024,256]{1,0:T(8,128)(2,1)} copy(bf16[1024,256]{1,0:T(8,128)(2,1)} %bitcast.6) | data formatting | bytes 1048576
